TPU v7x, 128 devices: a whole 4x4x4 slice. The times are simulated.
128 devices in a mesh: section: 4 (over z_lo, core), dir: 2 (over z_hi), dp: 16 (over y, x).
Axes of the slice: x: 4, y: 4, z: 4 (z_hi: 2, z_lo: 2; z = z_hi * 2 + z_lo), core: 2. Of those that a mesh axis runs over, the one named last changes fastest.
Arguments:
- acts: bfloat16 [2, 4, 2048, 4096], P('dir', 'section', 'dp'), may hold values from -6 to 6
- top_cot: bfloat16 [2, 2048, 4096], P('dir', 'dp'), may hold values from -3 to 3
- weights: bfloat16 [2, 4, 4096, 2048], P('dir', 'section', 'dp'), may hold values from -0.09375 to 0.09375
- gains: float32 [4, 4096], replicated, may hold values from 0.1 to 1.9
Outputs:
- grad_w: float32 [2, 4, 4096, 2048], P('dir', 'section', 'dp')
- out_cot: bfloat16 [2, 4, 2048, 4096], P('dir', 'section', 'dp')
All inputs are finite; a program needn't handle non-finite values.
Results may differ from a plain program's by a relative error of at most 0.02.
Values may be sent and summed in bfloat16 or wider, within the bound.
A program may use at most 192 MiB of HBM per device.

v0:
```python
import jax
import jax.numpy as jnp
from jax import lax
from jax.sharding import PartitionSpec as P

MICRO = 4


def swapped(value, axis, distance):
    mask = 2**distance
    pairs = [(source, source ^ mask) for source in range(lax.axis_size(axis))]
    return lax.ppermute(value, axis, pairs)


def padded(cells, sides, width):
    for axis, dim in sides:
        count = lax.axis_size(axis)
        ends = count - 1
        head = lax.slice_in_dim(cells, 0, width, axis=dim)
        tail = lax.slice_in_dim(cells, cells.shape[dim] - width, cells.shape[dim], axis=dim)
        cells = jnp.concatenate(
            [
                lax.ppermute(tail, axis, [(i, (i + 1) % count) for i in range(ends)]),
                cells,
                lax.ppermute(head, axis, [((i + 1) % count, i) for i in range(ends)]),
            ],
            axis=dim,
        )
    return cells


def to_partner(value):
    steps_bits = lax.axis_size("section").bit_length() - 1
    moved = swapped(value, "dir", 0)
    for bit in range(steps_bits):
        moved = swapped(moved, "section", bit)
    return moved


def slope_from(u_low):
    u_full = u_low.astype(jnp.float32)
    sig = jax.nn.sigmoid(u_full)
    return sig * (1.0 + u_full * (1.0 - sig))


def shards(acts, top_cot, weights, gains):
    inputs = acts[0, 0]
    top = top_cot[0]
    w_rows = weights[0, 0]
    total = inputs.shape[0]
    width = inputs.shape[1]
    half = w_rows.shape[1]
    block = total // MICRO
    segments = lax.axis_size("section")
    place = lax.axis_index("section")
    side = lax.axis_index("dir")
    depth = jnp.where(side == 0, segments - 1 - place, place)
    layer = segments - 1 - depth
    gain = lax.dynamic_slice_in_dim(gains, layer, 1, 0)[0]
    xf = inputs.astype(jnp.float32)
    scale = lax.rsqrt(jnp.mean(xf * xf, axis=-1, keepdims=True) + 1e-05)
    normed = xf * scale
    hn_me = (normed * gain).astype(jnp.bfloat16)
    w_mine = lax.all_gather(w_rows, "dp", axis=0, tiled=True)
    hn_partner = to_partner(hn_me)
    hn_both = jnp.concatenate([hn_me, hn_partner], axis=0)
    forward = jnp.dot(hn_both, w_mine, preferred_element_type=jnp.float32).astype(jnp.bfloat16)
    u_mine = forward[:total]
    u_back = to_partner(forward[total:])
    first = jnp.where(side == 0, u_mine, u_back)
    second = jnp.where(side == 0, u_back, u_mine)
    slope = slope_from(jnp.concatenate([first, second], axis=1))
    sent = jnp.zeros((block, width), jnp.bfloat16)
    out_rows = jnp.zeros((total, width), jnp.bfloat16)
    du_own = jnp.zeros((total, half), jnp.bfloat16)
    du_other = jnp.zeros((total, half), jnp.bfloat16)
    for step in range(segments + MICRO - 1):
        beside_all = padded(sent, (("section", 0),), block)
        incoming = jnp.where(side == 0, beside_all[2 * block :], beside_all[:block])
        micro = step - depth
        active = (micro >= 0) & (micro < MICRO)
        start = jnp.clip(micro, 0, MICRO - 1) * block
        from_top = lax.dynamic_slice_in_dim(top, start, block, 0)
        incoming = jnp.where(depth == 0, from_top, incoming)
        slope_now = lax.dynamic_slice_in_dim(slope, start, block, 0)
        du = (incoming.astype(jnp.float32) * slope_now).astype(jnp.bfloat16)
        du_split = du.reshape(block, 2, half)
        du_mine = jnp.where(side == 0, du_split[:, 0], du_split[:, 1])
        du_theirs = jnp.where(side == 0, du_split[:, 1], du_split[:, 0])
        du_recv = to_partner(du_theirs)
        stacked = jnp.concatenate([du_mine, du_recv], axis=0)
        prods = lax.dot_general(
            stacked, w_mine, (((1,), (1,)), ((), ())), preferred_element_type=jnp.float32
        ).astype(jnp.bfloat16)
        back = to_partner(prods[block:])
        dhn = prods[:block].astype(jnp.float32) + back.astype(jnp.float32)
        du_other = jnp.where(
            active, lax.dynamic_update_slice_in_dim(du_other, du_recv, start, 0), du_other
        )
        normed_now = lax.dynamic_slice_in_dim(normed, start, block, 0)
        scale_now = lax.dynamic_slice_in_dim(scale, start, block, 0)
        dyn = dhn * gain
        dxn = scale_now * (dyn - normed_now * jnp.mean(dyn * normed_now, axis=-1, keepdims=True))
        dx = (incoming.astype(jnp.float32) + dxn).astype(jnp.bfloat16)
        out_rows = jnp.where(
            active, lax.dynamic_update_slice_in_dim(out_rows, dx, start, 0), out_rows
        )
        du_own = jnp.where(
            active, lax.dynamic_update_slice_in_dim(du_own, du_mine, start, 0), du_own
        )
        sent = dx
    du_both = jnp.concatenate([du_own, du_other], axis=0)
    grad = lax.psum_scatter(
        lax.dot_general(
            hn_both, du_both, (((0,), (0,)), ((), ())), preferred_element_type=jnp.float32
        ).astype(jnp.bfloat16),
        "dp",
        scatter_dimension=0,
        tiled=True,
    ).astype(jnp.float32)
    return (grad[None, None], out_rows[None, None])


def solution(mesh):
    return jax.shard_map(
        shards,
        mesh=mesh,
        in_specs=(
            P("dir", "section", "dp", None),
            P("dir", "dp", None),
            P("dir", "section", "dp", None),
            P(),
        ),
        out_specs=(P("dir", "section", "dp", None), P("dir", "section", "dp", None)),
        check_vma=False,
    )
```

profile of v0, /device:TPU:0, one launch (start us, length us, event | category | flops | bytes accessed | tf_op | source)
XLA Modules:
  0.0 690.6 jit_solution(10313485045369002624)
XLA Ops:
  10.9 4.0 collective-permute-start
  14.9 23.2 %collective-permute-done = bf16[128,4096]{1,0:T(8,128)(2,1)S(1)} collective-permute-done((bf16[128,4096]{1,0:T(8,128)(2,1)S(1)}, bf16[128,4096]{1,0:T(8,128)(2,1)S(1)}, u32[]{:S(2)}, u32[]{:S(2)}) %collective-permute-start) | collective-permute-done | bytes 1048608 | tf_op jit(solution)/shard_map/ppermute | solution.py:12
  42.0 24.0 %collective-permute-done.2 = bf16[128,4096]{1,0:T(8,128)(2,1)} collective-permute-done((bf16[128,4096]{1,0:T(8,128)(2,1)S(1)}, bf16[128,4096]{1,0:T(8,128)(2,1)}, u32[]{:S(2)}, u32[]{:S(2)}) %collective-permute-start.2) | collective-permute-done | bytes 1048608 | tf_op jit(solution)/shard_map/ppermute | solution.py:12
  66.0 57.9 %all-gather.3.cloned.1.call-done = bf16[1,1,4096,2048]{3,2,1,0:T(8,128)(2,1)} async-done(((bf16[1,1,256,2048]{3,2,1,0:T(8,128)(2,1)}), bf16[1,1,4096,2048]{3,2,1,0:T(8,128)(2,1)}) %all-gather.3.cloned.1.call-update) | async-done | bytes 16777232 | tf_op jit(solution)/shard_map/all_gather | solution.py:64
  123.9 10.9 %fusion.37 = bf16[256,2048]{1,0:T(8,128)(2,1)S(1)} fusion(bf16[1,1,4096,2048]{3,2,1,0:T(8,128)(2,1)} %all-gather.3.cloned.1.call-done, bf16[128,4096]{1,0:T(8,128)(2,1)} %collective-permute-done.2, bf16[128,4096]{1,0:T(8,128)(2,1)} %copy-done.4), kind=kOutput, calls=%fused_computation.28 | convolution fusion | flops 4299685888 | bytes 19922944 | tf_op jit(solution)/shard_map/dot_general | solution.py:67
  138.1 12.0 %collective-permute-done.5 = bf16[128,2048]{1,0:T(8,128)(2,1)S(1)} collective-permute-done((bf16[128,2048]{1,0:T(8,128)(2,1)S(1)}, bf16[128,2048]{1,0:T(8,128)(2,1)S(1)}, u32[]{:S(2)}, u32[]{:S(2)}) %collective-permute-start.5) | collective-permute-done | bytes 524320 | tf_op jit(solution)/shard_map/ppermute | solution.py:12
  157.4 8.9 %collective-permute-done.7 = bf16[128,2048]{1,0:T(8,128)(2,1)} collective-permute-done((bf16[128,2048]{1,0:T(8,128)(2,1)}, bf16[128,2048]{1,0:T(8,128)(2,1)}, u32[]{:S(2)}, u32[]{:S(2)}) %collective-permute-start.7) | collective-permute-done | bytes 524320 | tf_op jit(solution)/shard_map/ppermute | solution.py:12
  186.3 11.0 %fusion.16 = bf16[64,4096]{1,0:T(8,128)(2,1)S(1)} fusion(bf16[1,1,4096,2048]{3,2,1,0:T(8,128)(2,1)} %all-gather.3.cloned.1.call-done, bf16[32,2048]{1,0:T(8,128)(2,1)S(1)} %collective-permute-done.10, bf16[32,2048]{1,0:T(8,128)(2,1)S(1)} %get-tuple-element.27), kind=kOutput, calls=%fused_computation.17 | convolution fusion | flops 1074528256 | bytes 17563648 | tf_op jit(solution)/shard_map/dot_general | solution.py:92
  200.3 6.5 collective-permute-done.11
  209.9 6.8 collective-permute-done.13
  220.9 3.8 collective-permute-done.14
  232.0 3.6 collective-permute-done.16
  246.7 11.9 %fusion.19 = bf16[64,4096]{1,0:T(8,128)(2,1)} fusion(bf16[1,1,4096,2048]{3,2,1,0:T(8,128)(2,1)} %all-gather.3.cloned.1.call-done, bf16[32,2048]{1,0:T(8,128)(2,1)} %copy-done.24, bf16[32,2048]{1,0:T(8,128)(2,1)} %get-tuple-element.25), kind=kOutput, calls=%fused_computation.18 | convolution fusion | flops 1074528256 | bytes 17563648 | tf_op jit(solution)/shard_map/dot_general | solution.py:92
  262.5 6.4 collective-permute-done.19
  271.2 7.6 %collective-permute-done.21 = bf16[32,4096]{1,0:T(8,128)(2,1)S(1)} collective-permute-done((bf16[32,4096]{1,0:T(8,128)(2,1)S(1)}, bf16[32,4096]{1,0:T(8,128)(2,1)S(1)}, u32[]{:S(2)}, u32[]{:S(2)}) %collective-permute-start.21) | collective-permute-done | bytes 262176 | tf_op jit(solution)/shard_map/ppermute | solution.py:12
  309.3 11.9 %fusion.22 = bf16[64,4096]{1,0:T(8,128)(2,1)} fusion(bf16[1,1,4096,2048]{3,2,1,0:T(8,128)(2,1)} %all-gather.3.cloned.1.call-done, bf16[32,2048]{1,0:T(8,128)(2,1)} %copy-done.26, bf16[32,2048]{1,0:T(8,128)(2,1)} %get-tuple-element.23), kind=kOutput, calls=%fused_computation.19 | convolution fusion | flops 1074528256 | bytes 17563648 | tf_op jit(solution)/shard_map/dot_general | solution.py:92
  325.2 6.4 collective-permute-done.27
  333.9 7.6 %collective-permute-done.29 = bf16[32,4096]{1,0:T(8,128)(2,1)S(1)} collective-permute-done((bf16[32,4096]{1,0:T(8,128)(2,1)S(1)}, bf16[32,4096]{1,0:T(8,128)(2,1)S(1)}, u32[]{:S(2)}, u32[]{:S(2)}) %collective-permute-start.29) | collective-permute-done | bytes 262176 | tf_op jit(solution)/shard_map/ppermute | solution.py:12
  371.7 11.9 %fusion.25 = bf16[64,4096]{1,0:T(8,128)(2,1)} fusion(bf16[1,1,4096,2048]{3,2,1,0:T(8,128)(2,1)} %all-gather.3.cloned.1.call-done, bf16[32,2048]{1,0:T(8,128)(2,1)} %copy-done.28, bf16[32,2048]{1,0:T(8,128)(2,1)} %get-tuple-element.21), kind=kOutput, calls=%fused_computation.20 | convolution fusion | flops 1074528256 | bytes 17563648 | tf_op jit(solution)/shard_map/dot_general | solution.py:92
  387.6 6.4 collective-permute-done.35
  396.3 7.6 %collective-permute-done.37 = bf16[32,4096]{1,0:T(8,128)(2,1)S(1)} collective-permute-done((bf16[32,4096]{1,0:T(8,128)(2,1)S(1)}, bf16[32,4096]{1,0:T(8,128)(2,1)S(1)}, u32[]{:S(2)}, u32[]{:S(2)}) %collective-permute-start.37) | collective-permute-done | bytes 262176 | tf_op jit(solution)/shard_map/ppermute | solution.py:12
  434.0 11.9 %fusion.28 = bf16[64,4096]{1,0:T(8,128)(2,1)} fusion(bf16[1,1,4096,2048]{3,2,1,0:T(8,128)(2,1)} %all-gather.3.cloned.1.call-done, bf16[32,2048]{1,0:T(8,128)(2,1)} %copy-done.30, bf16[32,2048]{1,0:T(8,128)(2,1)} %get-tuple-element.19), kind=kOutput, calls=%fused_computation.21 | convolution fusion | flops 1074528256 | bytes 17563648 | tf_op jit(solution)/shard_map/dot_general | solution.py:92
  449.9 6.4 collective-permute-done.43
  458.6 7.6 %collective-permute-done.45 = bf16[32,4096]{1,0:T(8,128)(2,1)S(1)} collective-permute-done((bf16[32,4096]{1,0:T(8,128)(2,1)S(1)}, bf16[32,4096]{1,0:T(8,128)(2,1)S(1)}, u32[]{:S(2)}, u32[]{:S(2)}) %collective-permute-start.45) | collective-permute-done | bytes 262176 | tf_op jit(solution)/shard_map/ppermute | solution.py:12
  496.5 11.9 %fusion.31 = bf16[64,4096]{1,0:T(8,128)(2,1)} fusion(bf16[1,1,4096,2048]{3,2,1,0:T(8,128)(2,1)} %all-gather.3.cloned.1.call-done, bf16[32,2048]{1,0:T(8,128)(2,1)} %copy-done.31, bf16[32,2048]{1,0:T(8,128)(2,1)} %get-tuple-element.17), kind=kOutput, calls=%fused_computation.22 | convolution fusion | flops 1074528256 | bytes 17563648 | tf_op jit(solution)/shard_map/dot_general | solution.py:92
  514.0 4.9 collective-permute-done.51
  522.8 6.3 collective-permute-done.53
  558.1 12.2 %convolution_convert_fusion = bf16[4096,2048]{1,0:T(8,128)(2,1)} fusion(bf16[128,4096]{1,0:T(8,128)(2,1)} %collective-permute-done.2, bf16[128,4096]{1,0:T(8,128)(2,1)} %copy-done.4, bf16[128,2048]{1,0:T(8,128)(2,1)} %select_dynamic-update-slice_fusion.6, bf16[128,2048]{1,0:T(8,128)(2,1)} %get-tuple-element.14), kind=kOutput, calls=%fused_computation.16 | convolution fusion | flops 4309647360 | bytes 19922944 | tf_op jit(solution)/shard_map/dot_general | solution.py:114
  570.3 11.7 %fusion.34 = bf16[64,4096]{1,0:T(8,128)(2,1)} fusion(bf16[1,1,4096,2048]{3,2,1,0:T(8,128)(2,1)} %all-gather.3.cloned.1.call-done, bf16[32,2048]{1,0:T(8,128)(2,1)S(1)} %collective-permute-done.58, bf16[32,2048]{1,0:T(8,128)(2,1)S(1)} %get-tuple-element.15), kind=kOutput, calls=%fused_computation.23 | convolution fusion | flops 1074528256 | bytes 17563648 | tf_op jit(solution)/shard_map/dot_general | solution.py:92
  586.0 6.0 collective-permute-done.59
  596.5 5.6 collective-permute-done.61
  603.3 77.2 %reduce-scatter.2.cloned.1.call-done = bf16[256,2048]{1,0:T(8,128)(2,1)} async-done(((bf16[4096,2048]{1,0:T(8,128)(2,1)}), bf16[256,2048]{1,0:T(8,128)(2,1)}) %reduce-scatter.2.cloned.1.call-update) | async-done | bytes 1048592 | tf_op jit(solution)/shard_map/reduce_scatter | solution.py:113
  (257 shorter events, 263.4 us)
Async XLA Ops:
  7.2 116.7 %all-gather.3.cloned.1.call-start = ((), (), s32[]{:S(2)}) async-start(), calls=%async_computation.2 | async-start | bytes 17825792 | tf_op jit(solution)/shard_map/all_gather | solution.py:64
  7.9 672.6 %reduce-scatter.2.cloned.1.call-start = ((), (), s32[]{:S(2)}) async-start(), calls=%async_computation.1 | async-start | bytes 17825792 | tf_op jit(solution)/shard_map/reduce_scatter | solution.py:113
  10.9 27.1 %collective-permute-start = (bf16[128,4096]{1,0:T(8,128)(2,1)S(1)}, bf16[128,4096]{1,0:T(8,128)(2,1)S(1)}, u32[]{:S(2)}, u32[]{:S(2)}) collective-permute-start(bf16[128,4096]{1,0:T(8,128)(2,1)S(1)} %get-tuple-element.45), channel_id=1, source_target_pairs={{0,16},{16,0},{1,17},{17,1},{2,18},{18,2},{3,19},{19,3},{4,20},{20... | collective-permute-start | bytes 3145736 | tf_op jit(solution)/shard_map/ppermute | solution.py:12
  40.7 25.3 %collective-permute-start.2 = (bf16[128,4096]{1,0:T(8,128)(2,1)S(1)}, bf16[128,4096]{1,0:T(8,128)(2,1)}, u32[]{:S(2)}, u32[]{:S(2)}) collective-permute-start(bf16[128,4096]{1,0:T(8,128)(2,1)S(1)} %collective-permute-done.1), channel_id=1, source_target_pairs={{0,64},{32,96},{64,0},{96,32},{1,65},{33,97},{65,1},{97,33},{2,66}... | collective-permute-start | bytes 3145736 | tf_op jit(solution)/shard_map/ppermute | solution.py:12
  134.8 15.2 %collective-permute-start.5 = (bf16[128,2048]{1,0:T(8,128)(2,1)S(1)}, bf16[128,2048]{1,0:T(8,128)(2,1)S(1)}, u32[]{:S(2)}, u32[]{:S(2)}) collective-permute-start(bf16[128,2048]{1,0:T(8,128)(2,1)S(1)} %slice.135), channel_id=1, source_target_pairs={{0,16},{16,0},{1,17},{17,1},{2,18},{18,2},{3,19},{19,3},{4,20},{20... | collective-permute-start | bytes 1572872 | tf_op jit(solution)/shard_map/ppermute | solution.py:12
  152.1 14.3 %collective-permute-start.7 = (bf16[128,2048]{1,0:T(8,128)(2,1)}, bf16[128,2048]{1,0:T(8,128)(2,1)}, u32[]{:S(2)}, u32[]{:S(2)}) collective-permute-start(bf16[128,2048]{1,0:T(8,128)(2,1)} %collective-permute-done.6), channel_id=1, source_target_pairs={{0,64},{32,96},{64,0},{96,32},{1,65},{33,97},{65,1},{97,33},{2,66}... | collective-permute-start | bytes 1572872 | tf_op jit(solution)/shard_map/ppermute | solution.py:12
  153.7 14.5 %collective-permute-start.4 = (bf16[32,4096]{1,0:T(8,128)(2,1)S(1)}, bf16[32,4096]{1,0:T(8,128)(2,1)}, u32[]{:S(2)}, u32[]{:S(2)}) collective-permute-start(bf16[32,4096]{1,0:T(8,128)(2,1)S(1)} %broadcast_in_dim.25), channel_id=1, source_target_pairs={{0,32},{32,64},{64,96},{1,33},{33,65},{65,97},{2,34},{34,66},{66,9... | collective-permute-start | bytes 786440 | tf_op jit(solution)/shard_map/ppermute | solution.py:23
  156.1 12.1 %collective-permute-start.3 = (bf16[32,4096]{1,0:T(8,128)(2,1)S(1)}, bf16[32,4096]{1,0:T(8,128)(2,1)}, u32[]{:S(2)}, u32[]{:S(2)}) collective-permute-start(bf16[32,4096]{1,0:T(8,128)(2,1)S(1)} %broadcast_in_dim.25), channel_id=1, source_target_pairs={{32,0},{64,32},{96,64},{33,1},{65,33},{97,65},{34,2},{66,34},{98,6... | collective-permute-start | bytes 786440 | tf_op jit(solution)/shard_map/ppermute | solution.py:25
  172.1 6.6 collective-permute-start.8
  180.0 6.4 collective-permute-start.10
  197.4 9.4 %collective-permute-start.11 = (bf16[32,4096]{1,0:T(8,128)(2,1)S(1)}, bf16[32,4096]{1,0:T(8,128)(2,1)S(1)}, u32[]{:S(2)}, u32[]{:S(2)}) collective-permute-start(bf16[32,4096]{1,0:T(8,128)(2,1)S(1)} %slice.139), channel_id=1, source_target_pairs={{0,16},{16,0},{1,17},{17,1},{2,18},{18,2},{3,19},{19,3},{4,20},{20... | collective-permute-start | bytes 786440 | tf_op jit(solution)/shard_map/ppermute | solution.py:12
  208.3 8.3 %collective-permute-start.13 = (bf16[32,4096]{1,0:T(8,128)(2,1)S(1)}, bf16[32,4096]{1,0:T(8,128)(2,1)S(1)}, u32[]{:S(2)}, u32[]{:S(2)}) collective-permute-start(bf16[32,4096]{1,0:T(8,128)(2,1)S(1)} %collective-permute-done.12), channel_id=1, source_target_pairs={{0,64},{32,96},{64,0},{96,32},{1,65},{33,97},{65,1},{97,33},{2,66}... | collective-permute-start | bytes 786440 | tf_op jit(solution)/shard_map/ppermute | solution.py:12
  229.1 6.6 collective-permute-start.16
  240.2 5.8 collective-permute-start.18
  259.6 9.3 %collective-permute-start.19 = (bf16[32,4096]{1,0:T(8,128)(2,1)S(1)}, bf16[32,4096]{1,0:T(8,128)(2,1)S(1)}, u32[]{:S(2)}, u32[]{:S(2)}) collective-permute-start(bf16[32,4096]{1,0:T(8,128)(2,1)S(1)} %slice.143), channel_id=1, source_target_pairs={{0,16},{16,0},{1,17},{17,1},{2,18},{18,2},{3,19},{19,3},{4,20},{20... | collective-permute-start | bytes 786440 | tf_op jit(solution)/shard_map/ppermute | solution.py:12
  270.4 8.3 %collective-permute-start.21 = (bf16[32,4096]{1,0:T(8,128)(2,1)S(1)}, bf16[32,4096]{1,0:T(8,128)(2,1)S(1)}, u32[]{:S(2)}, u32[]{:S(2)}) collective-permute-start(bf16[32,4096]{1,0:T(8,128)(2,1)S(1)} %collective-permute-done.20), channel_id=1, source_target_pairs={{0,64},{32,96},{64,0},{96,32},{1,65},{33,97},{65,1},{97,33},{2,66}... | collective-permute-start | bytes 786440 | tf_op jit(solution)/shard_map/ppermute | solution.py:12
  291.8 6.6 collective-permute-start.24
  322.2 9.3 %collective-permute-start.27 = (bf16[32,4096]{1,0:T(8,128)(2,1)S(1)}, bf16[32,4096]{1,0:T(8,128)(2,1)S(1)}, u32[]{:S(2)}, u32[]{:S(2)}) collective-permute-start(bf16[32,4096]{1,0:T(8,128)(2,1)S(1)} %slice.147), channel_id=1, source_target_pairs={{0,16},{16,0},{1,17},{17,1},{2,18},{18,2},{3,19},{19,3},{4,20},{20... | collective-permute-start | bytes 786440 | tf_op jit(solution)/shard_map/ppermute | solution.py:12
  333.1 8.3 %collective-permute-start.29 = (bf16[32,4096]{1,0:T(8,128)(2,1)S(1)}, bf16[32,4096]{1,0:T(8,128)(2,1)S(1)}, u32[]{:S(2)}, u32[]{:S(2)}) collective-permute-start(bf16[32,4096]{1,0:T(8,128)(2,1)S(1)} %collective-permute-done.28), channel_id=1, source_target_pairs={{0,64},{32,96},{64,0},{96,32},{1,65},{33,97},{65,1},{97,33},{2,66}... | collective-permute-start | bytes 786440 | tf_op jit(solution)/shard_map/ppermute | solution.py:12
  354.0 6.6 collective-permute-start.32
  365.2 5.9 collective-permute-start.34
  384.7 9.3 %collective-permute-start.35 = (bf16[32,4096]{1,0:T(8,128)(2,1)S(1)}, bf16[32,4096]{1,0:T(8,128)(2,1)S(1)}, u32[]{:S(2)}, u32[]{:S(2)}) collective-permute-start(bf16[32,4096]{1,0:T(8,128)(2,1)S(1)} %slice.151), channel_id=1, source_target_pairs={{0,16},{16,0},{1,17},{17,1},{2,18},{18,2},{3,19},{19,3},{4,20},{20... | collective-permute-start | bytes 786440 | tf_op jit(solution)/shard_map/ppermute | solution.py:12
  395.5 8.3 %collective-permute-start.37 = (bf16[32,4096]{1,0:T(8,128)(2,1)S(1)}, bf16[32,4096]{1,0:T(8,128)(2,1)S(1)}, u32[]{:S(2)}, u32[]{:S(2)}) collective-permute-start(bf16[32,4096]{1,0:T(8,128)(2,1)S(1)} %collective-permute-done.36), channel_id=1, source_target_pairs={{0,64},{32,96},{64,0},{96,32},{1,65},{33,97},{65,1},{97,33},{2,66}... | collective-permute-start | bytes 786440 | tf_op jit(solution)/shard_map/ppermute | solution.py:12
  416.4 6.6 collective-permute-start.40
  446.9 9.3 %collective-permute-start.43 = (bf16[32,4096]{1,0:T(8,128)(2,1)S(1)}, bf16[32,4096]{1,0:T(8,128)(2,1)S(1)}, u32[]{:S(2)}, u32[]{:S(2)}) collective-permute-start(bf16[32,4096]{1,0:T(8,128)(2,1)S(1)} %slice.155), channel_id=1, source_target_pairs={{0,16},{16,0},{1,17},{17,1},{2,18},{18,2},{3,19},{19,3},{4,20},{20... | collective-permute-start | bytes 786440 | tf_op jit(solution)/shard_map/ppermute | solution.py:12
  457.8 8.3 %collective-permute-start.45 = (bf16[32,4096]{1,0:T(8,128)(2,1)S(1)}, bf16[32,4096]{1,0:T(8,128)(2,1)S(1)}, u32[]{:S(2)}, u32[]{:S(2)}) collective-permute-start(bf16[32,4096]{1,0:T(8,128)(2,1)S(1)} %collective-permute-done.44), channel_id=1, source_target_pairs={{0,64},{32,96},{64,0},{96,32},{1,65},{33,97},{65,1},{97,33},{2,66}... | collective-permute-start | bytes 786440 | tf_op jit(solution)/shard_map/ppermute | solution.py:12
  478.9 6.6 collective-permute-start.48
  509.5 9.3 %collective-permute-start.51 = (bf16[32,4096]{1,0:T(8,128)(2,1)S(1)}, bf16[32,4096]{1,0:T(8,128)(2,1)S(1)}, u32[]{:S(2)}, u32[]{:S(2)}) collective-permute-start(bf16[32,4096]{1,0:T(8,128)(2,1)S(1)} %slice.159), channel_id=1, source_target_pairs={{0,16},{16,0},{1,17},{17,1},{2,18},{18,2},{3,19},{19,3},{4,20},{20... | collective-permute-start | bytes 786440 | tf_op jit(solution)/shard_map/ppermute | solution.py:12
  520.4 8.7 %collective-permute-start.53 = (bf16[32,4096]{1,0:T(8,128)(2,1)S(1)}, bf16[32,4096]{1,0:T(8,128)(2,1)S(1)}, u32[]{:S(2)}, u32[]{:S(2)}) collective-permute-start(bf16[32,4096]{1,0:T(8,128)(2,1)S(1)} %collective-permute-done.52), channel_id=1, source_target_pairs={{0,64},{32,96},{64,0},{96,32},{1,65},{33,97},{65,1},{97,33},{2,66}... | collective-permute-start | bytes 786440 | tf_op jit(solution)/shard_map/ppermute | solution.py:12
  539.1 6.6 collective-permute-start.56
  583.1 8.9 %collective-permute-start.59 = (bf16[32,4096]{1,0:T(8,128)(2,1)S(1)}, bf16[32,4096]{1,0:T(8,128)(2,1)S(1)}, u32[]{:S(2)}, u32[]{:S(2)}) collective-permute-start(bf16[32,4096]{1,0:T(8,128)(2,1)S(1)} %slice.163), channel_id=1, source_target_pairs={{0,16},{16,0},{1,17},{17,1},{2,18},{18,2},{3,19},{19,3},{4,20},{20... | collective-permute-start | bytes 786440 | tf_op jit(solution)/shard_map/ppermute | solution.py:12
  593.6 8.5 %collective-permute-start.61 = (bf16[32,4096]{1,0:T(8,128)(2,1)S(1)}, bf16[32,4096]{1,0:T(8,128)(2,1)S(1)}, u32[]{:S(2)}, u32[]{:S(2)}) collective-permute-start(bf16[32,4096]{1,0:T(8,128)(2,1)S(1)} %collective-permute-done.60), channel_id=1, source_target_pairs={{0,64},{32,96},{64,0},{96,32},{1,65},{33,97},{65,1},{97,33},{2,66}... | collective-permute-start | bytes 786440 | tf_op jit(solution)/shard_map/ppermute | solution.py:12
  (65 other events, 524.7 us)
Sparse Core Ops, SparseCore 0:
  10.2 113.6 all-gather.2
  570.4 109.9 reduce-scatter.1
where the time goes:
time: 699 us; the launch traced here: 691 us
  waiting for transfers between devices  375 us (54%)
  starting transfers between devices  111 us (16%)
  matrix products  105 us (15%)
  other arithmetic  56.9 us (8%)
  local copies, waits for them, and re-layouts  27.5 us (4%)
  between operations  15.2 us (2%)
    ppermute x48, waiting for transfers between devices, swapped(): return lax.ppermute(value, axis, pairs)  222 us
    ppermute x48, starting transfers between devices, swapped(): return lax.ppermute(value, axis, pairs)  90.3 us
    dot_general x7, matrix products, shards(): lax.dot_general(stacked, w_mine, (((1,), (1,)), ((), ())), preferred_elem...  82.4 us
    reduce_scatter x1, waiting for transfers between devices, shards(): lax.psum_scatter(lax.dot_general(hn_both, du_both, (((0,), (0,)), ((), ()...  77.2 us
    all_gather x1, waiting for transfers between devices, shards(): w_mine = lax.all_gather(w_rows, 'dp', axis=0, tiled=True)  57.9 us
    ppermute x7, waiting for transfers between devices, padded(): lax.ppermute(head, axis, [((i + 1) % count, i) for i in range(ends)])  17.5 us
  transfers between devices with their start and end apart: 64, of which 54 were waited for; matrix products, arithmetic and copies ran while one was open for 6% of the time, Pallas kernels for 0%

commit v1 on v0

v1 whole, which is shorter than its diff:
```python
import functools

import jax
import jax.numpy as jnp
from jax import lax
from jax.experimental import pallas as pl
from jax.experimental.pallas import tpu as pltpu
from jax.sharding import PartitionSpec as P

MESH = pl.DeviceIdType.MESH
MICRO = 4
F32 = jnp.float32
BF16 = jnp.bfloat16


def wait_bytes(ref, sem):
    pltpu.make_async_copy(ref, ref, sem).wait()


def kernel(
    micro, side, layers,
    x_ref, top_ref, w_ref, gains_ref,
    grad_ref, out_ref,
    hns, hnb, wb, up, ur, c_own, c_oth, dxb, dyn_s, du, pr, pp, gp, gr, scl,
    s_w, r_w, s_hn, s_hp, r_hn, s_u, r_u, s_c, r_c, s_d, r_d, s_po, s_pp, r_p, s_g, r_g, s_top, s_t, s_out,
):
    mb, width = x_ref.shape[1], x_ref.shape[2]
    half = w_ref.shape[1]
    kc = w_ref.shape[0]
    kb = kc * side
    chunks = side * side
    h = lax.axis_index("dir")
    place = lax.axis_index("section")
    g = lax.axis_index("dp")
    layer = jnp.where(h == 0, place, layers - 1 - place)
    even = lax.rem(layer, 2) == 0
    gy, gx = lax.div(g, side), lax.rem(g, side)
    i, j = jnp.where(even, gy, gx), jnp.where(even, gx, gy)
    sa = jnp.where(even, side, 1)
    sb = jnp.where(even, 1, side)

    def where_is(l, d, a, b):
        return {"section": jnp.where(d == 0, l, layers - 1 - l), "dir": d, "dp": a * sa + b * sb}

    def at_layer(l, d):
        return {"section": jnp.where(d == 0, l, layers - 1 - l), "dir": d, "dp": g}

    def other(v, step):
        return lax.rem(v + step, side)

    def send(src, dst, s, r, to):
        pltpu.make_async_remote_copy(
            src_ref=src, dst_ref=dst, send_sem=s, recv_sem=r, device_id=to, device_id_type=MESH
        ).start()

    below = lax.rem(layer + layers - 1, layers)
    above = lax.rem(layer + 1, layers)
    first = layer == layers - 1
    last = layer == 0

    def chunk_of(q):
        a, b = q // side, q % side
        iq, jq = jnp.where(even, a, b), jnp.where(even, b, a)
        return iq, pl.ds(pl.multiple_of(jq * kc, kc), kc)

    peers = []
    for step in range(1, side):
        peers.append(where_is(layer, h, other(i, step), j))
        peers.append(where_is(layer, h, i, other(j, step)))
    for step in range(side):
        peers.append(where_is(layer, 1 - h, other(i, step), j))
    for l in (below, above):
        for d in (h, 1 - h):
            peers.append(at_layer(l, d))
    barrier = pltpu.get_barrier_semaphore()
    for to in peers:
        pl.semaphore_signal(barrier, inc=1, device_id=to, device_id_type=MESH)
    pl.semaphore_wait(barrier, len(peers))

    for step in (2, 1, 3) if side == 4 else range(1, side):
        send(w_ref, wb.at[j], s_w, r_w, where_is(layer, h, i, other(j, step)))
    pltpu.make_async_copy(w_ref, wb.at[j], r_w).start()

    @pl.when(first)
    def _():
        for m in range(micro):
            for n in range(2):
                pltpu.make_async_copy(
                    top_ref.at[m, :, pl.ds(n * half, half)], c_own.at[m, n], s_top
                ).start()

    gain_row = pl.ds(layer, 1)

    def norm_step(m, carry):
        xf = x_ref[m].astype(F32)
        scale = lax.rsqrt(jnp.mean(xf * xf, axis=-1, keepdims=True) + 1e-05)
        scl[m] = jnp.broadcast_to(scale, (mb, 128))
        for q in range(chunks):
            iq, cols = chunk_of(q)
            xq = x_ref[m, :, q * kc : (q + 1) * kc].astype(F32)
            hns[iq, m, :, cols] = (xq * scale * gains_ref[gain_row, q * kc : (q + 1) * kc]).astype(BF16)
        return carry

    lax.fori_loop(0, micro, norm_step, 0)
    for step in range(side):
        to = other(i, step)
        send(hns.at[to], hnb.at[:, i, h], s_hp, r_hn, where_is(layer, 1 - h, to, j))
        if step:
            send(hns.at[to], hnb.at[:, i, h], s_hn, r_hn, where_is(layer, h, to, j))
        else:
            pltpu.make_async_copy(hns.at[i], hnb.at[:, i, h], r_hn).start()

    @pl.when(first)
    def _():
        wait_bytes(c_own, s_top)
        for m in range(micro):
            send(c_own.at[m, 1 - h], c_oth.at[m], s_t.at[m], r_c.at[m, 1], at_layer(layer, 1 - h))

    wait_bytes(wb, r_w)
    wait_bytes(hnb, r_hn)

    tile = min(512, half)

    def fwd_step(m, carry):
        rows = hnb[m].reshape(side * 2 * mb, kb)
        for n in range(half // tile):
            cols = slice(n * tile, (n + 1) * tile)
            part = jnp.dot(rows, wb[:, :, cols].reshape(kb, tile), preferred_element_type=F32)
            up[m, :, :, :, cols] = part.astype(BF16).reshape(side, 2, mb, tile)
        for step in range(1, side):
            to = other(i, step)
            send(up.at[m, to], ur.at[m, i], s_u.at[m], r_u.at[m], where_is(layer, h, to, j))
        return carry

    lax.fori_loop(0, micro, fwd_step, 0)

    def du_step(m):
        wait_bytes(ur.at[m, pl.ds(0, side - 1)], r_u.at[m])

        @pl.when(jnp.logical_not(first))
        def _():
            wait_bytes(c_own.at[m], r_c.at[m, 0])

        wait_bytes(c_oth.at[m], r_c.at[m, 1])
        for n in range(half // tile):
            cols = slice(n * tile, (n + 1) * tile)
            for mine in range(2):
                r = h if mine else 1 - h
                u = up[m, i, r, :, cols].astype(F32)
                for step in range(1, side):
                    u = u + ur[m, other(i, step), r, :, cols].astype(F32)
                sig = jax.nn.sigmoid(u)
                slope = sig * (1.0 + u * (1.0 - sig))
                c = c_own[m, h, :, cols] if mine else c_oth[m, :, cols]
                du[m, i, r, :, cols] = (c.astype(F32) * slope).astype(BF16)
        for step in range(1, side):
            to = other(i, step)
            send(du.at[m, i], du.at[m, i], s_d.at[m], r_d.at[m], where_is(layer, h, to, j))

    def prod_step(m):
        wait_bytes(du.at[m, pl.ds(0, side - 1)], r_d.at[m])
        rows = du[m].reshape(side * 2 * mb, half)
        for k in range(side):
            part = lax.dot_general(rows, wb[k], (((1,), (1,)), ((), ())), preferred_element_type=F32)
            pr[m, :, :, :, k * kc : (k + 1) * kc] = part.astype(BF16).reshape(side, 2, mb, kc)
        for step in range(side):
            to = other(i, step)
            send(pr.at[m, to, 1 - h], pp.at[m, h, i], s_pp.at[m], r_p.at[m], where_is(layer, 1 - h, to, j))
            if step:
                send(pr.at[m, to, h], pp.at[m, h, i], s_po.at[m], r_p.at[m], where_is(layer, h, to, j))
            else:
                pltpu.make_async_copy(pr.at[m, i, h], pp.at[m, h, i], r_p.at[m]).start()

    def dx_step(m):
        wait_bytes(pp.at[m], r_p.at[m])
        scale = scl[m][:, :1]
        total = jnp.zeros((mb, kc), F32)
        for q in range(chunks):
            iq, cols = chunk_of(q)
            nat = slice(q * kc, (q + 1) * kc)
            dhn = pp[m, 0, iq, :, cols].astype(F32) + pp[m, 1, iq, :, cols].astype(F32)
            dyn = dhn * gains_ref[gain_row, nat]
            dyn_s[:, nat] = dyn
            total = total + dyn * (x_ref[m, :, nat].astype(F32) * scale)
        mean = jnp.sum(total, axis=-1, keepdims=True) * (1.0 / width)
        per = chunks // 2
        for q in range(chunks):
            nat = slice(q * kc, (q + 1) * kc)
            low = slice((q % per) * kc, (q % per + 1) * kc)
            normed = x_ref[m, :, nat].astype(F32) * scale
            dxn = scale * (dyn_s[:, nat] - normed * mean)
            dxb[m, q // per, :, low] = (c_own[m, q // per, :, low].astype(F32) + dxn).astype(BF16)

        @pl.when(jnp.logical_not(last))
        def _():
            send(dxb.at[m], c_own.at[m], s_c.at[m, 0], r_c.at[m, 0], at_layer(below, h))
            send(dxb.at[m, 1 - h], c_oth.at[m], s_c.at[m, 1], r_c.at[m, 1], at_layer(below, 1 - h))

        for n in range(2):
            pltpu.make_async_copy(dxb.at[m, n], out_ref.at[m, :, pl.ds(n * half, half)], s_out).start()

    def chain_step(t, carry):
        pl.when(t < micro)(lambda: du_step(t))
        pl.when((t >= 1) & (t < micro + 1))(lambda: prod_step(t - 1))
        pl.when(t >= 2)(lambda: dx_step(t - 2))
        return carry

    lax.fori_loop(0, micro + 2, chain_step, 0)

    def grad_block(b, n):
        cols = slice(n * tile, (n + 1) * tile)
        lhs = hnb[:, :, :, :, pl.ds(pl.multiple_of(b * kc, kc), kc)].reshape(micro * side * 2 * mb, kc)
        rhs = du[:, :, :, :, cols].reshape(micro * side * 2 * mb, tile)
        return lax.dot_general(lhs, rhs, (((0,), (0,)), ((), ())), preferred_element_type=F32)

    for slot, step in enumerate((2, 1, 3) if side == 4 else range(1, side)):
        to = other(j, step)
        for n in range(half // tile):
            gp[slot, :, n * tile : (n + 1) * tile] = grad_block(to, n).astype(BF16)
        send(gp.at[slot], gr.at[j], s_g, r_g, where_is(layer, h, i, to))
    for n in range(half // tile):
        grad_ref[:, n * tile : (n + 1) * tile] = grad_block(j, n)
    wait_bytes(gr.at[pl.ds(0, side - 1)], r_g)
    for n in range(half // tile):
        cols = slice(n * tile, (n + 1) * tile)
        total = grad_ref[:, cols]
        for step in range(1, side):
            total = total + gr[other(j, step), :, cols].astype(F32)
        grad_ref[:, cols] = total

    wait_bytes(wb.at[pl.ds(0, side - 1)], s_w)
    wait_bytes(hns.at[pl.ds(0, side - 1)], s_hn)
    wait_bytes(hns, s_hp)
    wait_bytes(gp, s_g)
    wait_bytes(dxb, s_out)

    def drain(m, carry):
        wait_bytes(up.at[m, pl.ds(0, side - 1)], s_u.at[m])
        wait_bytes(du.at[m, pl.ds(0, side - 1)], s_d.at[m])
        wait_bytes(pr.at[m, pl.ds(0, side - 1), 0], s_po.at[m])
        wait_bytes(pr.at[m, :, 0], s_pp.at[m])

        @pl.when(first)
        def _():
            wait_bytes(c_oth.at[m], s_t.at[m])

        @pl.when(jnp.logical_not(last))
        def _():
            wait_bytes(dxb.at[m], s_c.at[m, 0])
            wait_bytes(dxb.at[m, 0], s_c.at[m, 1])

        return carry

    lax.fori_loop(0, micro, drain, 0)


def shards(acts, top_cot, weights, gains):
    tokens, width = acts.shape[2], acts.shape[3]
    rows, half = weights.shape[2], weights.shape[3]
    layers = lax.axis_size("section")
    parts = lax.axis_size("dp")
    side = int(round(parts**0.5))
    micro = MICRO
    mb = tokens // micro
    kb = rows * side
    dma = pltpu.SemaphoreType.DMA
    vmem = pl.BlockSpec(memory_space=pltpu.VMEM)
    hbm = pl.BlockSpec(memory_space=pl.ANY)
    grad, out = pl.pallas_call(
        functools.partial(kernel, micro, side, layers),
        out_shape=(
            jax.ShapeDtypeStruct((rows, half), F32),
            jax.ShapeDtypeStruct((micro, mb, width), BF16),
        ),
        in_specs=[vmem, hbm, vmem, vmem],
        out_specs=(vmem, hbm),
        scratch_shapes=[
            pltpu.VMEM((side, micro, mb, kb), BF16),
            pltpu.VMEM((micro, side, 2, mb, kb), BF16),
            pltpu.VMEM((side, rows, half), BF16),
            pltpu.VMEM((micro, side, 2, mb, half), BF16),
            pltpu.VMEM((micro, side, 2, mb, half), BF16),
            pltpu.VMEM((micro, 2, mb, half), BF16),
            pltpu.VMEM((micro, mb, half), BF16),
            pltpu.VMEM((micro, 2, mb, half), BF16),
            pltpu.VMEM((mb, width), F32),
            pltpu.VMEM((micro, side, 2, mb, half), BF16),
            pltpu.VMEM((micro, side, 2, mb, kb), BF16),
            pltpu.VMEM((micro, 2, side, mb, kb), BF16),
            pltpu.VMEM((side - 1, rows, half), BF16),
            pltpu.VMEM((side, rows, half), BF16),
            pltpu.VMEM((micro, mb, 128), F32),
            dma, dma, dma, dma, dma,
            dma((micro,)), dma((micro,)),
            dma((micro, 2)), dma((micro, 2)),
            dma((micro,)), dma((micro,)),
            dma((micro,)), dma((micro,)), dma((micro,)),
            dma, dma, dma, dma((micro,)), dma,
        ],
        compiler_params=pltpu.CompilerParams(
            collective_id=0, has_side_effects=True, vmem_limit_bytes=60 * 1024 * 1024
        ),
        cost_estimate=pl.CostEstimate(
            flops=12 * tokens * width * half, bytes_accessed=8 * rows * half, transcendentals=0
        ),
    )(
        acts.reshape(micro, mb, width),
        top_cot.reshape(micro, mb, width),
        weights.reshape(rows, half),
        gains,
    )
    return grad[None, None], out.reshape(1, 1, tokens, width)


def solution(mesh):
    return jax.shard_map(
        shards,
        mesh=mesh,
        in_specs=(
            P("dir", "section", "dp", None),
            P("dir", "dp", None),
            P("dir", "section", "dp", None),
            P(),
        ),
        out_specs=(P("dir", "section", "dp", None), P("dir", "section", "dp", None)),
        check_vma=False,
    )
```

time: 699 us -> 264 us (0.38); the launches traced: 691 us -> 264 us
  waiting for transfers between devices: 375 us -> 0 us
  Pallas kernels: 0 us -> 259 us
  starting transfers between devices: 111 us -> 0 us
  matrix products: 105 us -> 0 us
  other arithmetic: 56.9 us -> 0 us
  local copies, waits for them, and re-layouts: 27.5 us -> 4.2 us
  between operations: 15.2 us -> 0.65 us
    pallas_call x0 -> x1, Pallas kernels: none -> 259 us  [shards(): pl.pallas_call(functools.partial(kernel, micro, side, layers), out_shape=...]
    ppermute x62 -> x0, waiting for transfers between devices: 239 us -> none  [the longest x48 222 us: swapped(): return lax.ppermute(value, axis, pairs)]
    ppermute x62 -> x0, starting transfers between devices: 111 us -> none  [the longest x48 90.3 us: swapped(): return lax.ppermute(value, axis, pairs)]
    dot_general x9 -> x0, matrix products: 105 us -> none  [the longest x7 82.4 us: shards(): lax.dot_general(stacked, w_mine, (((1,), (1,)), ((), ())), preferred_elem...]
    reduce_scatter x1 -> x0, waiting for transfers between devices: 77.2 us -> none  [shards(): lax.psum_scatter(lax.dot_general(hn_both, du_both, (((0,), (0,)), ((), ()...]
    all_gather x1 -> x0, waiting for transfers between devices: 57.9 us -> none  [shards(): w_mine = lax.all_gather(w_rows, 'dp', axis=0, tiled=True)]
    select_n x29 -> x0, other arithmetic: 32.2 us -> none  [the longest x7 12.3 us: shards(): jnp.where(active, lax.dynamic_update_slice_in_dim(du_own, du_mine, start,...]
    convert_element_type x7 -> x0, other arithmetic: 14 us -> none  [shards(): du = (incoming.astype(jnp.float32) * slope_now).astype(jnp.bfloat16)]
  transfers between devices with their start and end apart: 64 -> 0, of which waited for: 54 -> 0; matrix products, arithmetic and copies ran while one was open for 6% -> 0% of each run, Pallas kernels for 0% -> 0%
where the time goes in v1:
time: 264 us
  Pallas kernels  259 us (98%)
  local copies, waits for them, and re-layouts  4.2 us (2%)
    pallas_call x1, Pallas kernels, shards(): pl.pallas_call(functools.partial(kernel, micro, side, layers), out_shape=...  259 us

profile of v1, /device:TPU:0, one launch (start us, length us, event | category | flops | bytes accessed | tf_op | source)
XLA Modules:
  0.0 264.1 jit_solution(8996246689699919188)
XLA Ops:
  0.6 259.3 %shard_map.59 = (f32[256,2048]{1,0:T(8,128)}, bf16[4,32,4096]{2,1,0:T(8,128)(2,1)}) custom-call(bf16[4,32,4096]{2,1,0:T(8,128)(2,1)} %bitcast.7, bf16[4,32,4096]{2,1,0:T(8,128)(2,1)} %bitcast.8, bf16[256,2048]{1,0:T(8,128)(2,1)} %bitcast.9, f32[4,4096]{1,0:T(4,128)} %gains_ref.1), custom_call_target="tpu_custom_call" | custom-call | flops 12884901888 | bytes 4194304 | tf_op jit(solution)/shard_map/pallas_call | solution.py:269
  259.9 0.0 copy-start
  259.9 3.2 %copy.8 = f32[1,1,256,2048]{3,2,1,0:T(8,128)} copy(f32[1,1,256,2048]{3,2,1,0:T(8,128)} %bitcast.5) | data formatting | bytes 4194304
  263.1 0.0 copy-done
  263.2 1.0 copy.9
Async XLA Ops:
  259.9 3.2 %copy-start = (bf16[4,32,4096]{2,1,0:T(8,128)(2,1)S(1)}, bf16[4,32,4096]{2,1,0:T(8,128)(2,1)}, u32[]{:S(2)}) copy-start(bf16[4,32,4096]{2,1,0:T(8,128)(2,1)} %get-tuple-element.5) | copy-start | bytes 3145732

commit v2 on v1

--- a/solution.py
+++ b/solution.py
@@ -8,7 +8,7 @@
 from jax.sharding import PartitionSpec as P
 
 MESH = pl.DeviceIdType.MESH
-MICRO = 4
+MICRO = 8
 F32 = jnp.float32
 BF16 = jnp.bfloat16
 
@@ -22,7 +22,7 @@
     x_ref, top_ref, w_ref, gains_ref,
     grad_ref, out_ref,
     hns, hnb, wb, up, ur, c_own, c_oth, dxb, dyn_s, du, pr, pp, gp, gr, scl,
-    s_w, r_w, s_hn, s_hp, r_hn, s_u, r_u, s_c, r_c, s_d, r_d, s_po, s_pp, r_p, s_g, r_g, s_top, s_t, s_out,
+    s_w, r_w, s_hn, s_hp, r_hn, s_u, r_u, s_c, r_c, s_d, r_d, s_po, s_pp, r_p, s_g, r_g, s_top, s_t, s_out, turn,
 ):
     mb, width = x_ref.shape[1], x_ref.shape[2]
     half = w_ref.shape[1]
@@ -213,10 +213,18 @@
         rhs = du[:, :, :, :, cols].reshape(micro * side * 2 * mb, tile)
         return lax.dot_general(lhs, rhs, (((0,), (0,)), ((), ())), preferred_element_type=F32)
 
-    for slot, step in enumerate((2, 1, 3) if side == 4 else range(1, side)):
+    order = (2, 1, 3) if side == 4 else range(1, side)
+
+    @pl.when(even)
+    def _():
+        pl.semaphore_signal(turn, inc=1, device_id=at_layer(above, h), device_id_type=MESH)
+
+    for slot, step in enumerate(order):
         to = other(j, step)
         for n in range(half // tile):
             gp[slot, :, n * tile : (n + 1) * tile] = grad_block(to, n).astype(BF16)
+        if slot == 0:
+            pl.when(jnp.logical_not(even))(lambda: pl.semaphore_wait(turn, 1))
         send(gp.at[slot], gr.at[j], s_g, r_g, where_is(layer, h, i, to))
     for n in range(half // tile):
         grad_ref[:, n * tile : (n + 1) * tile] = grad_block(j, n)
@@ -296,6 +304,7 @@
             dma((micro,)), dma((micro,)),
             dma((micro,)), dma((micro,)), dma((micro,)),
             dma, dma, dma, dma((micro,)), dma,
+            pltpu.SemaphoreType.REGULAR,
         ],
         compiler_params=pltpu.CompilerParams(
             collective_id=0, has_side_effects=True, vmem_limit_bytes=60 * 1024 * 1024

time: 264 us -> 207 us (0.78)
  Pallas kernels: 259 us -> 202 us
    pallas_call x1, Pallas kernels: 259 us -> 202 us  [shards(): pl.pallas_call(functools.partial(kernel, micro, side, layers), out_shape=...]
where the time goes in v2:
time: 207 us
  Pallas kernels  202 us (98%)
  local copies, waits for them, and re-layouts  4.2 us (2%)
    pallas_call x1, Pallas kernels, shards(): pl.pallas_call(functools.partial(kernel, micro, side, layers), out_shape=...  202 us
    unnamed x4, local copies, waits for them, and re-layouts  4.2 us

profile of v2, /device:TPU:0, one launch (start us, length us, event | category | flops | bytes accessed | tf_op | source)
XLA Modules:
  0.0 206.6 jit_solution(15930541500533060394)
XLA Ops:
  0.6 201.8 %shard_map.59 = (f32[256,2048]{1,0:T(8,128)}, bf16[8,16,4096]{2,1,0:T(8,128)(2,1)}) custom-call(bf16[8,16,4096]{2,1,0:T(8,128)(2,1)} %bitcast.7, bf16[8,16,4096]{2,1,0:T(8,128)(2,1)} %bitcast.8, bf16[256,2048]{1,0:T(8,128)(2,1)} %bitcast.9, f32[4,4096]{1,0:T(4,128)} %gains_ref.1), custom_call_target="tpu_custom_call" | custom-call | flops 12884901888 | bytes 4194304 | tf_op jit(solution)/shard_map/pallas_call | solution.py:277
  202.4 0.0 copy-start
  202.4 3.2 %copy.8 = f32[1,1,256,2048]{3,2,1,0:T(8,128)} copy(f32[1,1,256,2048]{3,2,1,0:T(8,128)} %bitcast.5) | data formatting | bytes 4194304
  205.6 0.0 copy-done
  205.6 1.0 copy.9
Async XLA Ops:
  202.4 3.2 %copy-start = (bf16[8,16,4096]{2,1,0:T(8,128)(2,1)S(1)}, bf16[8,16,4096]{2,1,0:T(8,128)(2,1)}, u32[]{:S(2)}) copy-start(bf16[8,16,4096]{2,1,0:T(8,128)(2,1)} %get-tuple-element.5) | copy-start | bytes 3145732

commit v3 on v1

--- a/solution.py
+++ b/solution.py
@@ -8,7 +8,7 @@
 from jax.sharding import PartitionSpec as P
 
 MESH = pl.DeviceIdType.MESH
-MICRO = 4
+MICRO = 8
 F32 = jnp.float32
 BF16 = jnp.bfloat16
 
@@ -19,14 +19,14 @@
 
 def kernel(
     micro, side, layers,
-    x_ref, top_ref, w_ref, gains_ref,
-    grad_ref, out_ref,
-    hns, hnb, wb, up, ur, c_own, c_oth, dxb, dyn_s, du, pr, pp, gp, gr, scl,
-    s_w, r_w, s_hn, s_hp, r_hn, s_u, r_u, s_c, r_c, s_d, r_d, s_po, s_pp, r_p, s_g, r_g, s_top, s_t, s_out,
+    x_hbm, top_ref, w_hbm, gains_ref,
+    own_ref, gr, out_ref,
+    x_ref, hns, hnb, wb, up, ur, ul, c_own, c_oth, dxb, dyn_s, du, pr, pp, gp, gl, gown, scl,
+    s_w, r_w, s_hn, s_hp, r_hn, s_u, r_u, r_ul, s_c, r_c, s_d, r_d, s_po, s_pp, r_p, s_g, r_g, r_gl, s_own, s_top, s_t, s_out, s_in, turn, ready,
 ):
     mb, width = x_ref.shape[1], x_ref.shape[2]
-    half = w_ref.shape[1]
-    kc = w_ref.shape[0]
+    half = w_hbm.shape[1]
+    kc = w_hbm.shape[0]
     kb = kc * side
     chunks = side * side
     h = lax.axis_index("dir")
@@ -47,6 +47,12 @@
 
     def other(v, step):
         return lax.rem(v + step, side)
+
+    i_right, i_far, i_left = other(i, 1), other(i, 2), other(i, 3)
+    j_right, j_far, j_left = other(j, 1), other(j, 2), other(j, 3)
+    a_right, a_left = where_is(layer, h, i_right, j), where_is(layer, h, i_left, j)
+    b_right, b_left = where_is(layer, h, i, j_right), where_is(layer, h, i, j_left)
+    low, high = pl.ds(0, kc // 2), pl.ds(kc // 2, kc // 2)
 
     def send(src, dst, s, r, to):
         pltpu.make_async_remote_copy(
@@ -75,11 +81,10 @@
     barrier = pltpu.get_barrier_semaphore()
     for to in peers:
         pl.semaphore_signal(barrier, inc=1, device_id=to, device_id_type=MESH)
-    pl.semaphore_wait(barrier, len(peers))
-
-    for step in (2, 1, 3) if side == 4 else range(1, side):
-        send(w_ref, wb.at[j], s_w, r_w, where_is(layer, h, i, other(j, step)))
-    pltpu.make_async_copy(w_ref, wb.at[j], r_w).start()
+    load_x = pltpu.make_async_copy(x_hbm, x_ref, s_in.at[0])
+    load_x.start()
+    load_w = pltpu.make_async_copy(w_hbm, wb.at[j], s_in.at[1])
+    load_w.start()
 
     @pl.when(first)
     def _():
@@ -101,7 +106,33 @@
             hns[iq, m, :, cols] = (xq * scale * gains_ref[gain_row, q * kc : (q + 1) * kc]).astype(BF16)
         return carry
 
+    load_x.wait()
     lax.fori_loop(0, micro, norm_step, 0)
+    load_w.wait()
+    pl.semaphore_wait(barrier, len(peers))
+
+    def pass_w(slot, part, sem, to):
+        send(wb.at[slot, part], wb.at[slot, part], s_w, r_w.at[sem], to)
+
+    def got_w(slot, part, sem):
+        wait_bytes(wb.at[slot, part], r_w.at[sem])
+
+    pass_w(j, low, 0, b_right)
+    pass_w(j, high, 2, b_left)
+    pass_w(j, high, 1, b_right)
+    pass_w(j, low, 3, b_left)
+
+    def relay_w():
+        got_w(j_left, low, 0)
+        pass_w(j_left, low, 4, b_right)
+        got_w(j_right, high, 2)
+        pass_w(j_right, high, 5, b_left)
+
+    @pl.when(even)
+    def _():
+        relay_w()
+        pl.semaphore_wait(ready, 1)
+
     for step in range(side):
         to = other(i, step)
         send(hns.at[to], hnb.at[:, i, h], s_hp, r_hn, where_is(layer, 1 - h, to, j))
@@ -116,26 +147,42 @@
         for m in range(micro):
             send(c_own.at[m, 1 - h], c_oth.at[m], s_t.at[m], r_c.at[m, 1], at_layer(layer, 1 - h))
 
-    wait_bytes(wb, r_w)
+    pl.when(jnp.logical_not(even))(relay_w)
+    got_w(j_left, high, 1)
+    got_w(j_right, low, 3)
+    got_w(j_far, low, 4)
+    got_w(j_far, high, 5)
+
+    @pl.when(jnp.logical_not(even))
+    def _():
+        pl.semaphore_signal(ready, inc=1, device_id=at_layer(below, h), device_id_type=MESH)
+
     wait_bytes(hnb, r_hn)
 
     tile = min(512, half)
 
-    def fwd_step(m, carry):
+    def fwd_step(m):
         rows = hnb[m].reshape(side * 2 * mb, kb)
         for n in range(half // tile):
             cols = slice(n * tile, (n + 1) * tile)
             part = jnp.dot(rows, wb[:, :, cols].reshape(kb, tile), preferred_element_type=F32)
             up[m, :, :, :, cols] = part.astype(BF16).reshape(side, 2, mb, tile)
-        for step in range(1, side):
-            to = other(i, step)
-            send(up.at[m, to], ur.at[m, i], s_u.at[m], r_u.at[m], where_is(layer, h, to, j))
-        return carry
-
-    lax.fori_loop(0, micro, fwd_step, 0)
+        send(up.at[m, i_far, 0], ul.at[m, 0], s_u.at[m], r_ul.at[m, 0], a_right)
+        send(up.at[m, i_far, 1], ul.at[m, 1], s_u.at[m], r_ul.at[m, 1], a_left)
+        send(up.at[m, i_right, 1], ur.at[m, 0, 1], s_u.at[m], r_u.at[m], a_right)
+        send(up.at[m, i_left, 0], ur.at[m, 1, 0], s_u.at[m], r_u.at[m], a_left)
+
+    def relay_step(m):
+        for r, (to, dev) in enumerate(((i_right, a_right), (i_left, a_left))):
+            wait_bytes(ul.at[m, r], r_ul.at[m, r])
+            for n in range(half // tile):
+                cols = slice(n * tile, (n + 1) * tile)
+                part = up[m, to, r, :, cols].astype(F32) + ul[m, r, :, cols].astype(F32)
+                up[m, to, r, :, cols] = part.astype(BF16)
+            send(up.at[m, to, r], ur.at[m, r, r], s_u.at[m], r_u.at[m], dev)
 
     def du_step(m):
-        wait_bytes(ur.at[m, pl.ds(0, side - 1)], r_u.at[m])
+        wait_bytes(ur.at[m], r_u.at[m])
 
         @pl.when(jnp.logical_not(first))
         def _():
@@ -147,8 +194,7 @@
             for mine in range(2):
                 r = h if mine else 1 - h
                 u = up[m, i, r, :, cols].astype(F32)
-                for step in range(1, side):
-                    u = u + ur[m, other(i, step), r, :, cols].astype(F32)
+                u = u + ur[m, 0, r, :, cols].astype(F32) + ur[m, 1, r, :, cols].astype(F32)
                 sig = jax.nn.sigmoid(u)
                 slope = sig * (1.0 + u * (1.0 - sig))
                 c = c_own[m, h, :, cols] if mine else c_oth[m, :, cols]
@@ -199,13 +245,19 @@
         for n in range(2):
             pltpu.make_async_copy(dxb.at[m, n], out_ref.at[m, :, pl.ds(n * half, half)], s_out).start()
 
-    def chain_step(t, carry):
-        pl.when(t < micro)(lambda: du_step(t))
-        pl.when((t >= 1) & (t < micro + 1))(lambda: prod_step(t - 1))
-        pl.when(t >= 2)(lambda: dx_step(t - 2))
+    lag = 2
+    begin = jnp.where(first, lag + 1, micro + lag)
+
+    def step_at(t, carry):
+        c = t - begin
+        pl.when(t < micro)(lambda: fwd_step(t))
+        pl.when((t >= lag) & (t < micro + lag))(lambda: relay_step(t - lag))
+        pl.when((c >= 0) & (c < micro))(lambda: du_step(c))
+        pl.when((c >= 1) & (c < micro + 1))(lambda: prod_step(c - 1))
+        pl.when(c >= 2)(lambda: dx_step(c - 2))
         return carry
 
-    lax.fori_loop(0, micro + 2, chain_step, 0)
+    lax.fori_loop(0, begin + micro + 2, step_at, 0)
 
     def grad_block(b, n):
         cols = slice(n * tile, (n + 1) * tile)
@@ -213,20 +265,35 @@
         rhs = du[:, :, :, :, cols].reshape(micro * side * 2 * mb, tile)
         return lax.dot_general(lhs, rhs, (((0,), (0,)), ((), ())), preferred_element_type=F32)
 
-    for slot, step in enumerate((2, 1, 3) if side == 4 else range(1, side)):
-        to = other(j, step)
+    def grad_part(slot, b):
         for n in range(half // tile):
-            gp[slot, :, n * tile : (n + 1) * tile] = grad_block(to, n).astype(BF16)
-        send(gp.at[slot], gr.at[j], s_g, r_g, where_is(layer, h, i, to))
+            gp[slot, :, n * tile : (n + 1) * tile] = grad_block(b, n).astype(BF16)
+
+    @pl.when(even)
+    def _():
+        pl.semaphore_signal(turn, inc=1, device_id=at_layer(above, h), device_id_type=MESH)
+
+    grad_part(0, j_far)
+    pl.when(jnp.logical_not(even))(lambda: pl.semaphore_wait(turn, 1))
+    send(gp.at[0, low], gl.at[0], s_g, r_gl.at[0], b_right)
+    send(gp.at[0, high], gl.at[1], s_g, r_gl.at[1], b_left)
+    grad_part(1, j_right)
+    send(gp.at[1, high], gr.at[0, high], s_g, r_g, b_right)
+    grad_part(2, j_left)
+    send(gp.at[2, low], gr.at[1, low], s_g, r_g, b_left)
     for n in range(half // tile):
-        grad_ref[:, n * tile : (n + 1) * tile] = grad_block(j, n)
-    wait_bytes(gr.at[pl.ds(0, side - 1)], r_g)
-    for n in range(half // tile):
-        cols = slice(n * tile, (n + 1) * tile)
-        total = grad_ref[:, cols]
-        for step in range(1, side):
-            total = total + gr[other(j, step), :, cols].astype(F32)
-        grad_ref[:, cols] = total
+        gown[:, n * tile : (n + 1) * tile] = grad_block(j, n)
+    store_own = pltpu.make_async_copy(gown, own_ref, s_own)
+    store_own.start()
+    for side_way, (rows, dev) in enumerate(((low, b_right), (high, b_left))):
+        wait_bytes(gl.at[side_way], r_gl.at[side_way])
+        for n in range(half // tile):
+            cols = slice(n * tile, (n + 1) * tile)
+            part = gp[1 + side_way, rows, cols].astype(F32) + gl[side_way, :, cols].astype(F32)
+            gp[1 + side_way, rows, cols] = part.astype(BF16)
+        send(gp.at[1 + side_way, rows], gr.at[side_way, rows], s_g, r_g, dev)
+    wait_bytes(gr, r_g)
+    store_own.wait()
 
     wait_bytes(wb.at[pl.ds(0, side - 1)], s_w)
     wait_bytes(hns.at[pl.ds(0, side - 1)], s_hn)
@@ -266,20 +333,23 @@
     dma = pltpu.SemaphoreType.DMA
     vmem = pl.BlockSpec(memory_space=pltpu.VMEM)
     hbm = pl.BlockSpec(memory_space=pl.ANY)
-    grad, out = pl.pallas_call(
+    own, parts_in, out = pl.pallas_call(
         functools.partial(kernel, micro, side, layers),
         out_shape=(
             jax.ShapeDtypeStruct((rows, half), F32),
+            jax.ShapeDtypeStruct((2, rows, half), BF16),
             jax.ShapeDtypeStruct((micro, mb, width), BF16),
         ),
-        in_specs=[vmem, hbm, vmem, vmem],
-        out_specs=(vmem, hbm),
+        in_specs=[hbm, hbm, hbm, vmem],
+        out_specs=(hbm, hbm, hbm),
         scratch_shapes=[
+            pltpu.VMEM((micro, mb, width), BF16),
             pltpu.VMEM((side, micro, mb, kb), BF16),
             pltpu.VMEM((micro, side, 2, mb, kb), BF16),
             pltpu.VMEM((side, rows, half), BF16),
             pltpu.VMEM((micro, side, 2, mb, half), BF16),
-            pltpu.VMEM((micro, side, 2, mb, half), BF16),
+            pltpu.VMEM((micro, 2, 2, mb, half), BF16),
+            pltpu.VMEM((micro, 2, mb, half), BF16),
             pltpu.VMEM((micro, 2, mb, half), BF16),
             pltpu.VMEM((micro, mb, half), BF16),
             pltpu.VMEM((micro, 2, mb, half), BF16),
@@ -288,14 +358,18 @@
             pltpu.VMEM((micro, side, 2, mb, kb), BF16),
             pltpu.VMEM((micro, 2, side, mb, kb), BF16),
             pltpu.VMEM((side - 1, rows, half), BF16),
-            pltpu.VMEM((side, rows, half), BF16),
+            pltpu.VMEM((2, rows // 2, half), BF16),
+            pltpu.VMEM((rows, half), F32),
             pltpu.VMEM((micro, mb, 128), F32),
-            dma, dma, dma, dma, dma,
-            dma((micro,)), dma((micro,)),
+            dma, dma((6,)), dma, dma, dma,
+            dma((micro,)), dma((micro,)), dma((micro, 2)),
             dma((micro, 2)), dma((micro, 2)),
             dma((micro,)), dma((micro,)),
             dma((micro,)), dma((micro,)), dma((micro,)),
-            dma, dma, dma, dma((micro,)), dma,
+            dma, dma, dma((2,)), dma,
+            dma, dma((micro,)), dma,
+            dma((2,)),
+            pltpu.SemaphoreType.REGULAR, pltpu.SemaphoreType.REGULAR,
         ],
         compiler_params=pltpu.CompilerParams(
             collective_id=0, has_side_effects=True, vmem_limit_bytes=60 * 1024 * 1024
@@ -309,6 +383,7 @@
         weights.reshape(rows, half),
         gains,
     )
+    grad = own + parts_in[0].astype(F32) + parts_in[1].astype(F32)
     return grad[None, None], out.reshape(1, 1, tokens, width)
 
 

time: 264 us -> 178 us (0.67)
  Pallas kernels: 259 us -> 173 us
  other arithmetic: 0 us -> 4.07 us
  local copies, waits for them, and re-layouts: 4.2 us -> 0.97 us
    pallas_call x1, Pallas kernels: 259 us -> 173 us  [shards(): pl.pallas_call(functools.partial(kernel, micro, side, layers), out_shape=...]
    broadcast_in_dim x0 -> x1, other arithmetic: none -> 4.07 us  [shards(): return (grad[None, None], out.reshape(1, 1, tokens, width))]
    unnamed x4 -> x3, local copies, waits for them, and re-layouts: 4.2 us -> 0.97 us
where the time goes in v3:
time: 178 us
  Pallas kernels  173 us (97%)
  other arithmetic  4.07 us (2%)
    pallas_call x1, Pallas kernels, shards(): pl.pallas_call(functools.partial(kernel, micro, side, layers), out_shape=...  173 us
    broadcast_in_dim x1, other arithmetic, shards(): return (grad[None, None], out.reshape(1, 1, tokens, width))  4.07 us

profile of v3, /device:TPU:0, one launch (start us, length us, event | category | flops | bytes accessed | tf_op | source)
XLA Modules:
  0.0 178.2 jit_solution(10166348956798732742)
XLA Ops:
  0.6 172.5 %shard_map.59 = (f32[256,2048]{1,0:T(8,128)}, bf16[2,256,2048]{2,1,0:T(8,128)(2,1)}, bf16[8,16,4096]{2,1,0:T(8,128)(2,1)}) custom-call(bf16[8,16,4096]{2,1,0:T(8,128)(2,1)} %bitcast.13, bf16[8,16,4096]{2,1,0:T(8,128)(2,1)} %bitcast.14, bf16[256,2048]{1,0:T(8,128)(2,1)} %bitcast.15, f32[4,4096]{1,0:T(4,128)} %gains_ref.1), custom_call_target="tpu_custom_call" | custom-call | flops 12884901888 | bytes 4194304 | tf_op jit(solution)/shard_map/pallas_call | solution.py:336
  173.2 0.0 copy-start
  173.2 4.1 %fusion = f32[1,1,256,2048]{3,2,1,0:T(8,128)} fusion(f32[256,2048]{1,0:T(8,128)} %get-tuple-element.5, bf16[2,256,2048]{2,1,0:T(8,128)(2,1)} %get-tuple-element.6), kind=kLoop, calls=%fused_computation.1 | loop fusion | flops 2097152 | bytes 6291456 | tf_op jit(solution)/shard_map/broadcast_in_dim | solution.py:387
  177.2 0.0 copy-done
  177.2 1.0 copy.7
Async XLA Ops:
  173.2 4.1 %copy-start = (bf16[8,16,4096]{2,1,0:T(8,128)(2,1)S(1)}, bf16[8,16,4096]{2,1,0:T(8,128)(2,1)}, u32[]{:S(2)}) copy-start(bf16[8,16,4096]{2,1,0:T(8,128)(2,1)} %get-tuple-element.7) | copy-start | bytes 3145732

commit v4 on v3

--- a/solution.py
+++ b/solution.py
@@ -257,7 +257,9 @@
         pl.when(c >= 2)(lambda: dx_step(c - 2))
         return carry
 
-    lax.fori_loop(0, begin + micro + 2, step_at, 0)
+    lax.fori_loop(0, begin + micro + 1, step_at, 0)
+
+    pl.when(jnp.logical_not(last))(lambda: dx_step(micro - 1))
 
     def grad_block(b, n):
         cols = slice(n * tile, (n + 1) * tile)
@@ -281,6 +283,7 @@
     send(gp.at[1, high], gr.at[0, high], s_g, r_g, b_right)
     grad_part(2, j_left)
     send(gp.at[2, low], gr.at[1, low], s_g, r_g, b_left)
+    pl.when(last)(lambda: dx_step(micro - 1))
     for n in range(half // tile):
         gown[:, n * tile : (n + 1) * tile] = grad_block(j, n)
     store_own = pltpu.make_async_copy(gown, own_ref, s_own)
@@ -319,6 +322,35 @@
         return carry
 
     lax.fori_loop(0, micro, drain, 0)
+
+
+def finish(own_hbm, parts_hbm, out_hbm, grad_hbm, res_hbm, own, parts, out, s_own, s_parts, s_out, s_grad, s_res):
+    count = s_own.shape[0]
+    rows = own.shape[0] // count
+    def at(k):
+        return pl.ds(k * rows, rows)
+    loads = []
+    for k in range(count):
+        loads.append((
+            pltpu.make_async_copy(own_hbm.at[at(k)], own.at[at(k)], s_own.at[k]),
+            pltpu.make_async_copy(parts_hbm.at[:, at(k)], parts.at[:, at(k)], s_parts.at[k]),
+        ))
+        for copy in loads[-1]:
+            copy.start()
+    load_out = pltpu.make_async_copy(out_hbm, out, s_out)
+    load_out.start()
+    stores = []
+    for k in range(count):
+        for copy in loads[k]:
+            copy.wait()
+        own[at(k)] = own[at(k)] + parts[0, at(k)].astype(F32) + parts[1, at(k)].astype(F32)
+        stores.append(pltpu.make_async_copy(own.at[at(k)], grad_hbm.at[at(k)], s_grad.at[k]))
+        stores[-1].start()
+    load_out.wait()
+    stores.append(pltpu.make_async_copy(out, res_hbm, s_res))
+    stores[-1].start()
+    for copy in stores:
+        copy.wait()
 
 
 def shards(acts, top_cot, weights, gains):
@@ -383,7 +415,24 @@
         weights.reshape(rows, half),
         gains,
     )
-    grad = own + parts_in[0].astype(F32) + parts_in[1].astype(F32)
+    count = 4
+    grad, out = pl.pallas_call(
+        finish,
+        out_shape=(
+            jax.ShapeDtypeStruct((rows, half), F32),
+            jax.ShapeDtypeStruct((micro, mb, width), BF16),
+        ),
+        in_specs=[hbm, hbm, hbm],
+        out_specs=(hbm, hbm),
+        scratch_shapes=[
+            pltpu.VMEM((rows, half), F32),
+            pltpu.VMEM((2, rows, half), BF16),
+            pltpu.VMEM((micro, mb, width), BF16),
+            dma((count,)), dma((count,)), dma, dma((count,)), dma,
+        ],
+        compiler_params=pltpu.CompilerParams(vmem_limit_bytes=60 * 1024 * 1024),
+        cost_estimate=pl.CostEstimate(flops=2 * rows * half, bytes_accessed=20 * rows * half, transcendentals=0),
+    )(own, parts_in, out)
     return grad[None, None], out.reshape(1, 1, tokens, width)
 
 

time: 178 us -> 173 us (0.972)
  other arithmetic: 4.07 us -> 0 us
    pallas_call x1, Pallas kernels: 173 us -> 168 us  [shards(): pl.pallas_call(functools.partial(kernel, micro, side, layers), out_shape=...]
    broadcast_in_dim x1 -> x0, other arithmetic: 4.07 us -> none  [shards(): return (grad[None, None], out.reshape(1, 1, tokens, width))]
    pallas_call x0 -> x1, Pallas kernels: none -> 4.04 us  [shards(): pl.pallas_call(finish, out_shape=(jax.ShapeDtypeStruct((rows, half), F32)...]
where the time goes in v4:
time: 173 us; the launch traced here: 172 us
  Pallas kernels  172 us (99%)
    pallas_call x1, Pallas kernels, shards(): pl.pallas_call(functools.partial(kernel, micro, side, layers), out_shape=...  168 us
    pallas_call x1, Pallas kernels, shards(): pl.pallas_call(finish, out_shape=(jax.ShapeDtypeStruct((rows, half), F32)...  4.04 us

profile of v4, /device:TPU:0, one launch (start us, length us, event | category | flops | bytes accessed | tf_op | source)
XLA Modules:
  0.0 172.4 jit_solution(4985367786457014215)
XLA Ops:
  0.6 167.7 %shard_map.59 = (f32[256,2048]{1,0:T(8,128)}, bf16[2,256,2048]{2,1,0:T(8,128)(2,1)}, bf16[8,16,4096]{2,1,0:T(8,128)(2,1)}) custom-call(bf16[8,16,4096]{2,1,0:T(8,128)(2,1)} %bitcast.6, bf16[8,16,4096]{2,1,0:T(8,128)(2,1)} %bitcast.7, bf16[256,2048]{1,0:T(8,128)(2,1)} %bitcast.8, f32[4,4096]{1,0:T(4,128)} %gains_ref.1), custom_call_target="tpu_custom_call" | custom-call | flops 12884901888 | bytes 4194304 | tf_op jit(solution)/shard_map/pallas_call | solution.py:368
  168.4 4.0 %shard_map.60 = (f32[256,2048]{1,0:T(8,128)}, bf16[8,16,4096]{2,1,0:T(8,128)(2,1)}) custom-call(f32[256,2048]{1,0:T(8,128)} %get-tuple-element.7.own_hbm, bf16[2,256,2048]{2,1,0:T(8,128)(2,1)} %get-tuple-element.8.parts_hbm, bf16[8,16,4096]{2,1,0:T(8,128)(2,1)} %get-tuple-element.9.out_hbm), custom_call_target="tpu_custom_call" | custom-call | flops 1048576 | bytes 10485760 | tf_op jit(solution)/shard_map/pallas_call | solution.py:419

commit v5 on v4

--- a/solution.py
+++ b/solution.py
@@ -199,23 +199,25 @@
                 slope = sig * (1.0 + u * (1.0 - sig))
                 c = c_own[m, h, :, cols] if mine else c_oth[m, :, cols]
                 du[m, i, r, :, cols] = (c.astype(F32) * slope).astype(BF16)
-        for step in range(1, side):
+        for step in (2, 1, 3):
             to = other(i, step)
             send(du.at[m, i], du.at[m, i], s_d.at[m], r_d.at[m], where_is(layer, h, to, j))
 
     def prod_step(m):
         wait_bytes(du.at[m, pl.ds(0, side - 1)], r_d.at[m])
         rows = du[m].reshape(side * 2 * mb, half)
-        for k in range(side):
-            part = lax.dot_general(rows, wb[k], (((1,), (1,)), ((), ())), preferred_element_type=F32)
-            pr[m, :, :, :, k * kc : (k + 1) * kc] = part.astype(BF16).reshape(side, 2, mb, kc)
-        for step in range(side):
-            to = other(i, step)
-            send(pr.at[m, to, 1 - h], pp.at[m, h, i], s_pp.at[m], r_p.at[m], where_is(layer, 1 - h, to, j))
-            if step:
-                send(pr.at[m, to, h], pp.at[m, h, i], s_po.at[m], r_p.at[m], where_is(layer, h, to, j))
-            else:
-                pltpu.make_async_copy(pr.at[m, i, h], pp.at[m, h, i], r_p.at[m]).start()
+        for part in range(2):
+            some = pl.ds(part * (kb // 2), kb // 2)
+            for k in range(part * side // 2, (part + 1) * side // 2):
+                prod = lax.dot_general(rows, wb[k], (((1,), (1,)), ((), ())), preferred_element_type=F32)
+                pr[m, :, :, :, k * kc : (k + 1) * kc] = prod.astype(BF16).reshape(side, 2, mb, kc)
+            for step in (2, 1, 3, 0):
+                to = other(i, step)
+                send(pr.at[m, to, 1 - h, :, some], pp.at[m, h, i, :, some], s_pp.at[m], r_p.at[m], where_is(layer, 1 - h, to, j))
+            for step in (2, 1, 3):
+                to = other(i, step)
+                send(pr.at[m, to, h, :, some], pp.at[m, h, i, :, some], s_po.at[m], r_p.at[m], where_is(layer, h, to, j))
+            pltpu.make_async_copy(pr.at[m, i, h, :, some], pp.at[m, h, i, :, some], r_p.at[m]).start()
 
     def dx_step(m):
         wait_bytes(pp.at[m], r_p.at[m])
@@ -261,9 +263,11 @@
 
     pl.when(jnp.logical_not(last))(lambda: dx_step(micro - 1))
 
-    def grad_block(b, n):
+    def grad_block(b, n, part=None):
         cols = slice(n * tile, (n + 1) * tile)
-        lhs = hnb[:, :, :, :, pl.ds(pl.multiple_of(b * kc, kc), kc)].reshape(micro * side * 2 * mb, kc)
+        size = kc if part is None else kc // 2
+        start = pl.multiple_of(b * kc + (part or 0) * size, size)
+        lhs = hnb[:, :, :, :, pl.ds(start, size)].reshape(micro * side * 2 * mb, size)
         rhs = du[:, :, :, :, cols].reshape(micro * side * 2 * mb, tile)
         return lax.dot_general(lhs, rhs, (((0,), (0,)), ((), ())), preferred_element_type=F32)
 
@@ -275,9 +279,14 @@
     def _():
         pl.semaphore_signal(turn, inc=1, device_id=at_layer(above, h), device_id_type=MESH)
 
-    grad_part(0, j_far)
+    def grad_half(b, part):
+        for n in range(half // tile):
+            gp[0, part * kc // 2 : (part + 1) * kc // 2, n * tile : (n + 1) * tile] = grad_block(b, n, part).astype(BF16)
+
+    grad_half(j_far, 0)
     pl.when(jnp.logical_not(even))(lambda: pl.semaphore_wait(turn, 1))
     send(gp.at[0, low], gl.at[0], s_g, r_gl.at[0], b_right)
+    grad_half(j_far, 1)
     send(gp.at[0, high], gl.at[1], s_g, r_gl.at[1], b_left)
     grad_part(1, j_right)
     send(gp.at[1, high], gr.at[0, high], s_g, r_g, b_right)

time: 173 us -> 171 us (0.988)
  Pallas kernels: 172 us -> 169 us
    pallas_call x1, Pallas kernels: 168 us -> 165 us  [shards(): pl.pallas_call(functools.partial(kernel, micro, side, layers), out_shape=...]
where the time goes in v5:
time: 171 us; the launch traced here: 170 us
  Pallas kernels  169 us (99%)
    pallas_call x1, Pallas kernels, shards(): pl.pallas_call(functools.partial(kernel, micro, side, layers), out_shape=...  165 us
    pallas_call x1, Pallas kernels, shards(): pl.pallas_call(finish, out_shape=(jax.ShapeDtypeStruct((rows, half), F32)...  4.04 us

profile of v5, /device:TPU:0, one launch (start us, length us, event | category | flops | bytes accessed | tf_op | source)
XLA Modules:
  0.0 170.1 jit_solution(17651972834100666078)
XLA Ops:
  0.6 165.4 %shard_map.59 = (f32[256,2048]{1,0:T(8,128)}, bf16[2,256,2048]{2,1,0:T(8,128)(2,1)}, bf16[8,16,4096]{2,1,0:T(8,128)(2,1)}) custom-call(bf16[8,16,4096]{2,1,0:T(8,128)(2,1)} %bitcast.6, bf16[8,16,4096]{2,1,0:T(8,128)(2,1)} %bitcast.7, bf16[256,2048]{1,0:T(8,128)(2,1)} %bitcast.8, f32[4,4096]{1,0:T(4,128)} %gains_ref.1), custom_call_target="tpu_custom_call" | custom-call | flops 12884901888 | bytes 4194304 | tf_op jit(solution)/shard_map/pallas_call | solution.py:377
  166.0 4.0 %shard_map.60 = (f32[256,2048]{1,0:T(8,128)}, bf16[8,16,4096]{2,1,0:T(8,128)(2,1)}) custom-call(f32[256,2048]{1,0:T(8,128)} %get-tuple-element.7.own_hbm, bf16[2,256,2048]{2,1,0:T(8,128)(2,1)} %get-tuple-element.8.parts_hbm, bf16[8,16,4096]{2,1,0:T(8,128)(2,1)} %get-tuple-element.9.out_hbm), custom_call_target="tpu_custom_call" | custom-call | flops 1048576 | bytes 10485760 | tf_op jit(solution)/shard_map/pallas_call | solution.py:428

commit v6 on v5

--- a/solution.py
+++ b/solution.py
@@ -241,8 +241,9 @@
 
         @pl.when(jnp.logical_not(last))
         def _():
-            send(dxb.at[m], c_own.at[m], s_c.at[m, 0], r_c.at[m, 0], at_layer(below, h))
             send(dxb.at[m, 1 - h], c_oth.at[m], s_c.at[m, 1], r_c.at[m, 1], at_layer(below, 1 - h))
+            for n in range(2):
+                send(dxb.at[m, n], c_own.at[m, n], s_c.at[m, 0], r_c.at[m, 0], at_layer(below, h))
 
         for n in range(2):
             pltpu.make_async_copy(dxb.at[m, n], out_ref.at[m, :, pl.ds(n * half, half)], s_out).start()

time: 171 us -> 169 us (0.988)
  no operation moved by 1% of the time
where the time goes in v6:
time: 169 us; the launch traced here: 168 us
  Pallas kernels  168 us (99%)
    pallas_call x1, Pallas kernels, shards(): pl.pallas_call(functools.partial(kernel, micro, side, layers), out_shape=...  164 us
    pallas_call x1, Pallas kernels, shards(): pl.pallas_call(finish, out_shape=(jax.ShapeDtypeStruct((rows, half), F32)...  4.04 us

profile of v6, /device:TPU:0, one launch (start us, length us, event | category | flops | bytes accessed | tf_op | source)
XLA Modules:
  0.0 168.5 jit_solution(6129837211026412401)
XLA Ops:
  0.6 163.8 %shard_map.59 = (f32[256,2048]{1,0:T(8,128)}, bf16[2,256,2048]{2,1,0:T(8,128)(2,1)}, bf16[8,16,4096]{2,1,0:T(8,128)(2,1)}) custom-call(bf16[8,16,4096]{2,1,0:T(8,128)(2,1)} %bitcast.6, bf16[8,16,4096]{2,1,0:T(8,128)(2,1)} %bitcast.7, bf16[256,2048]{1,0:T(8,128)(2,1)} %bitcast.8, f32[4,4096]{1,0:T(4,128)} %gains_ref.1), custom_call_target="tpu_custom_call" | custom-call | flops 12884901888 | bytes 4194304 | tf_op jit(solution)/shard_map/pallas_call | solution.py:378
  164.4 4.0 %shard_map.60 = (f32[256,2048]{1,0:T(8,128)}, bf16[8,16,4096]{2,1,0:T(8,128)(2,1)}) custom-call(f32[256,2048]{1,0:T(8,128)} %get-tuple-element.7.own_hbm, bf16[2,256,2048]{2,1,0:T(8,128)(2,1)} %get-tuple-element.8.parts_hbm, bf16[8,16,4096]{2,1,0:T(8,128)(2,1)} %get-tuple-element.9.out_hbm), custom_call_target="tpu_custom_call" | custom-call | flops 1048576 | bytes 10485760 | tf_op jit(solution)/shard_map/pallas_call | solution.py:429

commit v7 on v6

--- a/solution.py
+++ b/solution.py
@@ -241,7 +241,9 @@
 
         @pl.when(jnp.logical_not(last))
         def _():
-            send(dxb.at[m, 1 - h], c_oth.at[m], s_c.at[m, 1], r_c.at[m, 1], at_layer(below, 1 - h))
+            for n in range(2):
+                some = pl.ds(n * (half // 2), half // 2)
+                send(dxb.at[m, 1 - h, :, some], c_oth.at[m, :, some], s_c.at[m, 1], r_c.at[m, 1], at_layer(below, 1 - h))
             for n in range(2):
                 send(dxb.at[m, n], c_own.at[m, n], s_c.at[m, 0], r_c.at[m, 0], at_layer(below, h))
 

time: 169 us -> 169 us (level)
  no operation moved by 1% of the time
where the time goes in v7:
time: 169 us
  Pallas kernels  168 us (99%)
    pallas_call x1, Pallas kernels, shards(): pl.pallas_call(functools.partial(kernel, micro, side, layers), out_shape=...  164 us
    pallas_call x1, Pallas kernels, shards(): pl.pallas_call(finish, out_shape=(jax.ShapeDtypeStruct((rows, half), F32)...  4.04 us

profile of v7, /device:TPU:0, one launch (start us, length us, event | category | flops | bytes accessed | tf_op | source)
XLA Modules:
  0.0 168.5 jit_solution(16751250075654000342)
XLA Ops:
  0.6 163.9 %shard_map.59 = (f32[256,2048]{1,0:T(8,128)}, bf16[2,256,2048]{2,1,0:T(8,128)(2,1)}, bf16[8,16,4096]{2,1,0:T(8,128)(2,1)}) custom-call(bf16[8,16,4096]{2,1,0:T(8,128)(2,1)} %bitcast.6, bf16[8,16,4096]{2,1,0:T(8,128)(2,1)} %bitcast.7, bf16[256,2048]{1,0:T(8,128)(2,1)} %bitcast.8, f32[4,4096]{1,0:T(4,128)} %gains_ref.1), custom_call_target="tpu_custom_call" | custom-call | flops 12884901888 | bytes 4194304 | tf_op jit(solution)/shard_map/pallas_call | solution.py:380
  164.5 4.0 %shard_map.60 = (f32[256,2048]{1,0:T(8,128)}, bf16[8,16,4096]{2,1,0:T(8,128)(2,1)}) custom-call(f32[256,2048]{1,0:T(8,128)} %get-tuple-element.7.own_hbm, bf16[2,256,2048]{2,1,0:T(8,128)(2,1)} %get-tuple-element.8.parts_hbm, bf16[8,16,4096]{2,1,0:T(8,128)(2,1)} %get-tuple-element.9.out_hbm), custom_call_target="tpu_custom_call" | custom-call | flops 1048576 | bytes 10485760 | tf_op jit(solution)/shard_map/pallas_call | solution.py:431
